TPU v7x, 128 devices: a whole 4x4x4 slice. The times are simulated.
128 devices in a mesh: lat: 8 (over y_hi, x), lon: 16 (over z, y_lo, core).
Axes of the slice: x: 4, y: 4 (y_hi: 2, y_lo: 2; y = y_hi * 2 + y_lo), z: 4, core: 2. Of those that a mesh axis runs over, the one named last changes fastest.
Arguments:
- tokens: bfloat16 [1, 96, 768, 512], P(None, 'lat', 'lon'), may hold values from -6 to 6
- w_qkv_fine: bfloat16 [3, 512, 512], replicated
- w_proj_fine: bfloat16 [512, 512], replicated, may hold values from -0.25 to 0.25
- w_merge: bfloat16 [8192, 2048], P('lat'), may hold values from -0.0625 to 0.0625
- w_qkv_coarse: bfloat16 [3, 2048, 2048], P(None, None, 'lat')
- w_proj_coarse: bfloat16 [2048, 2048], P('lat'), may hold values from -0.125 to 0.125
- cot_fine: bfloat16 [1, 96, 768, 512], P(None, 'lat', 'lon'), may hold values from -6 to 6
- cot_coarse: bfloat16 [1, 24, 192, 2048], P(None, 'lat', 'lon'), may hold values from -6 to 6
Outputs:
- grad_tokens: bfloat16 [1, 96, 768, 512], P(None, 'lat', 'lon')
- grad_qkv_fine: float32 [3, 512, 512], replicated
- grad_proj_fine: float32 [512, 512], replicated
- grad_merge: float32 [8192, 2048], P('lat', 'lon')
- grad_qkv_coarse: float32 [3, 2048, 2048], P(None, 'lon', 'lat')
- grad_proj_coarse: float32 [2048, 2048], P('lat', 'lon')
All inputs are finite; a program needn't handle non-finite values.
Results may differ from a plain program's by a relative error of at most 0.038.
Values may be sent and summed in bfloat16 or wider, within the bound.
A program may use at most 128 MiB of HBM per device.

v0:
```python
import jax
import jax.numpy as jnp
import numpy as np
from jax import lax
from jax.experimental import pallas as pl
from jax.experimental.pallas import tpu as pltpu
from jax.sharding import PartitionSpec as P

MESH = pl.DeviceIdType.MESH
F32 = jnp.float32
BF16 = jnp.bfloat16
EPS = 1e-05
LATS = 8
ROWS, COLS = 12, 48
WL, WC = 6, 12
CELL = 40
WIN = 80
E = 512
HALO = ((0, 128), (128, 64), (192, 32))
VMEM_BYTES = 63 * 1024 * 1024


def tables():
    win = np.zeros((ROWS, COLS), np.int64)
    cell = np.zeros((ROWS, COLS), np.int64)
    for i in range(ROWS):
        for j in range(COLS):
            win[i, j] = ((i // WL) * 4 + j // WC) * WIN + (i % WL) * WC + j % WC
            cell[i, j] = ((i % 4) * 4 + j % 4) * CELL + (i // 4) * 12 + j // 4
    size = 16 * CELL
    to_cells = np.zeros((size, ROWS * COLS), np.float32)
    in_send = np.zeros((224, size), np.float32)
    in_own = np.zeros((size, size), np.float32)
    in_halo = np.zeros((size, 224), np.float32)
    out_send = np.zeros((224, size), np.float32)
    out_own = np.zeros((size, size), np.float32)
    out_halo = np.zeros((size, 224), np.float32)
    for i in range(ROWS):
        for j in range(COLS):
            to_cells[cell[i, j], i * COLS + j] = 1
            r, c = i + 3, j + 6
            if r < ROWS and c < COLS:
                in_own[win[i, j], cell[r, c]] = 1
                out_own[cell[r, c], win[i, j]] = 1
            else:
                if c < COLS:
                    slot = (r - ROWS) * 42 + c - 6
                elif r < ROWS:
                    slot = 128 + (r - 3) * 6 + c - COLS
                else:
                    slot = 192 + (r - ROWS) * 6 + c - COLS
                in_send[slot, cell[r % ROWS, c % COLS]] = 1
                in_halo[win[i, j], slot] = 1
                out_send[slot, win[i, j]] = 1
                out_halo[cell[r % ROWS, c % COLS], slot] = 1
    return [
        jnp.asarray(t, BF16)
        for t in (to_cells, in_send, in_own, in_halo, out_send, out_own, out_halo, to_cells.T)
    ]


def mm(a, b):
    return jnp.dot(a, b, preferred_element_type=F32)


def mm_nt(a, b):
    return lax.dot_general(a, b, (((1,), (1,)), ((), ())), preferred_element_type=F32)


def mm_tn(a, b):
    return lax.dot_general(a, b, (((0,), (0,)), ((), ())), preferred_element_type=F32)


def normalize(x):
    centred = x - jnp.mean(x, axis=-1, keepdims=True)
    return centred * lax.rsqrt(jnp.mean(centred * centred, axis=-1, keepdims=True) + EPS)


def pullback(x, dy):
    centred = x - jnp.mean(x, axis=-1, keepdims=True)
    rate = lax.rsqrt(jnp.mean(centred * centred, axis=-1, keepdims=True) + EPS)
    y = centred * rate
    inner = jnp.mean(dy * y, axis=-1, keepdims=True)
    return rate * (dy - jnp.mean(dy, axis=-1, keepdims=True) - y * inner)


def total(x, axes):
    s = jnp.sum(x, axis=-1, keepdims=True)
    return jnp.sum(s, axis=axes, keepdims=True)


def group_stats(x, axis, count):
    mean = total(x, axis) * (1.0 / count)
    centred = x - mean
    rate = lax.rsqrt(total(centred * centred, axis) * (1.0 / count) + EPS)
    return centred * rate, rate


def group_pullback(x, dy, axis, count):
    y, rate = group_stats(x, axis, count)
    inner = total(dy * y, axis) * (1.0 / count)
    return rate * (dy - total(dy, axis) * (1.0 / count) - y * inner)


def head_masks():
    lane = lax.broadcasted_iota(jnp.int32, (1, 256), 1) // 64
    return [jnp.where(lane == h, 1.0, 0.0) for h in range(4)]


def stack_heads(x, masks):
    return jnp.concatenate([x * m.astype(BF16) for m in masks], axis=0)


def pick_heads(x, masks):
    out = x[:WIN] * masks[0]
    for h in range(1, 4):
        out = out + x[h * WIN : (h + 1) * WIN] * masks[h]
    return out


def softmax_rows(scores):
    weights = jnp.exp(scores - jnp.max(scores, axis=-1, keepdims=True))
    return weights / jnp.sum(weights, axis=-1, keepdims=True)


def scores_back(probs, d_probs):
    d_probs = d_probs.astype(BF16).astype(F32)
    inner = jnp.sum(d_probs * probs, axis=-1, keepdims=True)
    return (probs * (d_probs - inner) * 0.125).astype(BF16)


def greet(devices):
    barrier = pltpu.get_barrier_semaphore()
    for device in devices:
        pl.semaphore_signal(barrier, inc=1, device_id=device, device_id_type=MESH)
    pl.semaphore_wait(barrier, len(devices))


def remote(src, dst, send, recv, device):
    return pltpu.make_async_remote_copy(
        src_ref=src, dst_ref=dst, send_sem=send, recv_sem=recv, device_id=device, device_id_type=MESH
    )


class Place:
    def __init__(self):
        self.lat = lax.axis_index("lat")
        self.lon = lax.axis_index("lon")

    def lat_peer(self, k):
        return lax.rem(self.lat + k, LATS)

    def at_lat(self, k):
        return (self.lat_peer(k), self.lon)

    def halo(self, step):
        up = lax.rem(self.lat + step + LATS, LATS)
        side = lax.rem(self.lon + step + 16, 16)
        return ((up, self.lon), (self.lat, side), (up, side))

    def lon_at(self, z, y, core):
        return (self.lat, z * 4 + y * 2 + core)


def start_halo(where, step, src, dst, sems):
    copies = []
    for n, device in enumerate(where.halo(step)):
        first, count = HALO[n]
        copies.append(
            remote(
                src.at[pl.ds(first, count)],
                dst.at[pl.ds(first, count)],
                sems.at[0, n],
                sems.at[1, n],
                device,
            )
        )
        copies[-1].start()
    return copies


def wait_all(copies):
    for copy in copies:
        copy.wait()


def start_spread(where, src_of, dst, sems):
    copies = []
    for k in range(1, LATS):
        copies.append(
            remote(
                src_of(where.lat_peer(k)),
                dst.at[where.lat],
                sems.at[0, k],
                sems.at[1, k],
                where.at_lat(k),
            )
        )
        copies[-1].start()
    return copies


def finish_spread(where, src_of, dst, sems):
    for k in range(1, LATS):
        source = where.lat_peer(LATS - k)
        remote(src_of(source), dst.at[source], sems.at[0, k], sems.at[1, k], where.at_lat(k)).wait()


def unpack(x):
    x = x.astype(F32)
    width = x.shape[-1]
    halves = [x[:, :CELL].reshape(LATS * CELL, width), x[:, CELL:].reshape(LATS * CELL, width)]
    return jnp.concatenate(halves, axis=1).astype(BF16)


def pack(top, bottom):
    width = top.shape[-1]
    halves = [top.reshape(LATS, CELL, width), bottom.reshape(LATS, CELL, width)]
    return jnp.concatenate(halves, axis=1).astype(BF16)


def swap_halves(x):
    low = lax.broadcasted_iota(jnp.int32, x.shape, 0) % 8 < 4
    count = x.shape[0]
    return jnp.where(low, pltpu.roll(x, count - 4, 0), pltpu.roll(x, 4, 0))


def fold(parts):
    n, _, width = parts[0].shape
    low = lax.broadcasted_iota(jnp.int32, (n * 8, width), 0) % 8 < 4
    pieces = [p[:, :32] for p in parts]
    for c in (0, 2):
        first = parts[c][:, 32:].reshape(n * 8, width)
        second = swap_halves(parts[c + 1][:, 32:].reshape(n * 8, width))
        pieces.append(jnp.where(low, first, second).reshape(n, 8, width))
    return jnp.concatenate(pieces, axis=1)


def unfold(x):
    n, _, width = x.shape
    low = lax.broadcasted_iota(jnp.int32, (n * 8, width), 0) % 8 < 4
    parts = []
    for c in range(4):
        tail = x[:, 128 + c // 2 * 8 : 136 + c // 2 * 8].reshape(n * 8, width)
        if c % 2:
            tail = swap_halves(tail)
        tail = jnp.where(low, tail, 0.0).reshape(n, 8, width)
        parts.append(jnp.concatenate([x[:, c * 32 : c * 32 + 32], tail], axis=1))
    return parts


def unfold_rows(x):
    parts = [p.reshape(LATS * CELL, 512) for p in unfold(x.astype(F32))]
    return jnp.concatenate(parts, axis=1).astype(BF16)


def unfold_one(x):
    return jnp.concatenate(unfold(x[None]), axis=0)


def fold_one(x):
    return fold([x[c : c + 1] for c in range(4)])[0]


class Flights:
    def __init__(self):
        self.open = {}

    def start(self, name, copies):
        self.open[name] = copies
        for copy in copies:
            copy.start()

    def wait(self, name):
        for copy in self.open.pop(name):
            copy.wait()


def spread(where, src_of, dst_of, sems):
    return [
        remote(
            src_of(where.lat_peer(k)), dst_of(where.lat), sems.at[0, k], sems.at[1, k], where.at_lat(k)
        )
        for k in range(1, LATS)
    ]


def halo_copies(where, step, src, dst, sems):
    copies = []
    for n, device in enumerate(where.halo(step)):
        rows = pl.ds(*HALO[n])
        copies.append(remote(src.at[rows], dst.at[rows], sems.at[0, n], sems.at[1, n], device))
    return copies


def sum_slots(ref):
    value = ref[0].astype(F32)
    for n in range(1, ref.shape[0]):
        value = value + ref[n].astype(F32)
    return value


def whole(
    cot_in, tokens_h, to_cells_h, in_send_h, in_own_h, in_halo_h,
    out_send_h, out_own_h, out_halo_h, to_grid_h, cot_fine_h,
    w_qkv_f_h, w_proj_f_h, w_merge_h, w_qkv_c_h, w_proj_c_h,
    grad_tokens, grad_qkv_f, grad_proj_f, grad_merge, grad_qkv_c, grad_proj_c,
    to_cells, in_send, in_own, in_halo, out_send, out_own, out_halo, to_grid, grid_in, w_qkv_f, w_proj_f, w_merge, w_qkv_c, w_proj_c,
    x, q, k, v, probs, mixed_f, tg, blended, merged, slices,
    send_in, got_in, send_out, got_out, got_in2, got_out2,
    cot, part, part_got, coarse_ref, packed, normed_got, rows, rows_t, cot_rows, qkv, d_mixed_c, mixed_c, d_qkv,
    d_packed, slices_t,
    share, core_a, z_a, line_a, y_a,
    core_b, z_b, line_b, y_b,
    fine_0, pair_0, lat_0, lon_0, piece_0, half_0, fine_1, pair_1, lat_1, lon_1, piece_1, half_1,
    load_sems, halo_sems, lat_sems, share_sems, z_sems, core_sems, lon_sems, pass_sems,
):
    where = Place()
    z, y, core = where.lon // 4, lax.rem(where.lon // 2, 2), lax.rem(where.lon, 2)
    chips = [(a, b) for a in range(4) for b in range(2)]
    around = [where.lon_at(lax.rem(z + a, 4), lax.rem(y + b, 2), core) for a, b in chips]
    sibling = where.lon_at(z, y, 1 - core)
    other_y = where.lon_at(z, 1 - y, core)
    flights = Flights()

    def body():
        barrier = pltpu.get_barrier_semaphore()
        friends = [where.at_lat(n) for n in range(1, LATS)] + around[1:] + [sibling]
        friends += list(where.halo(-1)[1:]) + list(where.halo(1)[1:])
        for device in friends:
            pl.semaphore_signal(barrier, inc=1, device_id=device, device_id_type=MESH)
        flights.start("tokens", [pltpu.make_async_copy(tokens_h, grid_in, load_sems.at[13])])
        loads = (
            ("to_cells", to_cells_h, to_cells), ("in_send", in_send_h, in_send),
            ("in_own", in_own_h, in_own), ("in_halo", in_halo_h, in_halo),
            ("w_qkv_f", w_qkv_f_h, w_qkv_f), ("w_proj_f", w_proj_f_h, w_proj_f),
            ("out_send", out_send_h, out_send), ("out_own", out_own_h, out_own),
            ("out_halo", out_halo_h, out_halo), ("w_merge", w_merge_h, w_merge),
            ("w_proj_c", w_proj_c_h, w_proj_c), ("w_qkv_c", w_qkv_c_h, w_qkv_c),
            ("to_grid", to_grid_h, to_grid),
        )
        for n, (name, far, near) in enumerate(loads):
            flights.start(name, [pltpu.make_async_copy(far, near, load_sems.at[n])])

        target = lax.broadcasted_iota(jnp.int32, (CELL, 12), 0)
        column = lax.broadcasted_iota(jnp.int32, (CELL, 12), 1)
        cot_wide = jnp.zeros((CELL, 2048), F32)
        for n in range(3):
            place = jnp.where(target == column + 12 * n, 1.0, 0.0).astype(BF16)
            cot_wide = cot_wide + mm(place, cot_in[n])
        cot[...] = fold([cot_wide[None, :, c * 512 : c * 512 + 512] for c in range(4)])[0].astype(BF16)
        flights.wait("tokens")
        flights.wait("to_cells")
        cells = mm(to_cells[...], grid_in[...])
        tg[...] = cells.astype(BF16)
        flights.start("cot_fine", [pltpu.make_async_copy(cot_fine_h, grid_in, load_sems.at[13])])
        normed = normalize(cells).astype(BF16)
        flights.wait("in_send")
        send_in[...] = mm(in_send[...], normed).astype(BF16)
        pl.semaphore_wait(barrier, len(friends))
        flights.start("halo1", halo_copies(where, -1, send_in, got_in, halo_sems.at[0]))
        flights.start("cots", spread(where, lambda peer: cot, lambda lat: normed_got.at[lat], lat_sems.at[0]))
        normed_got[where.lat] = cot[...]
        flights.wait("in_own")
        flights.wait("in_halo")
        own = mm(in_own[...], normed)
        flights.wait("halo1")
        x[...] = (own + mm(in_halo[...], got_in[...])).astype(BF16)
        flights.wait("w_qkv_f")
        for m, ref in enumerate((q, k, v)):
            ref[...] = mm(x[...], w_qkv_f[m]).astype(BF16)
        masks = head_masks()
        key = lax.broadcasted_iota(jnp.int32, (4 * WIN, WIN), 1)
        query = lax.broadcasted_iota(jnp.int32, (4 * WIN, WIN), 0) % WIN
        real = key < 72
        same = (key < 36) == (query < 36)
        last = where.lat == LATS - 1

        def window(w, carry):
            own_rows = pl.ds(pl.multiple_of(w * WIN, WIN), WIN)
            bound = jnp.logical_and(last, w >= 4)
            for g in range(2):
                lanes = slice(g * 256, g * 256 + 256)
                scores = mm_nt(stack_heads(q[own_rows, lanes], masks), k[own_rows, lanes]) * 0.125
                allowed = jnp.logical_and(real, jnp.logical_or(same, jnp.logical_not(bound)))
                weights = softmax_rows(jnp.where(allowed, scores, -1e30))
                probs[w * 2 + g] = weights
                mixed_f[own_rows, lanes] = pick_heads(
                    mm(weights.astype(BF16), v[own_rows, lanes]), masks
                ).astype(BF16)
            return carry

        lax.fori_loop(0, 8, window, 0, unroll=2)
        flights.wait("w_proj_f")
        out = mm(mixed_f[...], w_proj_f[...]).astype(BF16)
        flights.wait("out_send")
        send_out[...] = mm(out_send[...], out).astype(BF16)
        flights.start("halo2", halo_copies(where, 1, send_out, got_out, halo_sems.at[1]))
        flights.wait("out_own")
        flights.wait("out_halo")
        own = tg[...].astype(F32) + mm(out_own[...], out)
        flights.wait("halo2")
        blended[...] = own + mm(out_halo[...], got_out[...])
        merged[...] = (
            group_stats(blended[...].reshape(16, CELL, E), 0, 16 * E)[0]
            .reshape(LATS, WIN, E)
            .astype(BF16)
        )
        flights.start("merged", spread(where, lambda peer: merged.at[peer], lambda lat: slices.at[lat], lat_sems.at[1]))
        slices[where.lat] = merged[where.lat]
        flights.wait("cots")
        cot_rows[...] = unfold_rows(normed_got[...])
        flights.wait("w_proj_c")
        d_mixed_c[...] = mm_nt(cot_rows[...], w_proj_c[...]).astype(BF16)
        flights.wait("w_merge")
        flights.wait("merged")

        own_rows = unpack(slices[...])

        def merge(c, carry):
            quarters = []
            for n in range(4):
                lanes = pl.ds(pl.multiple_of(n * 512 + c * 256, 256), 256)
                quarters.append(mm(own_rows, w_merge[:, lanes]).reshape(LATS, CELL, 256))
            part[:, :, pl.ds(pl.multiple_of(c * 256, 256), 256)] = fold(quarters).astype(BF16)
            return carry

        def half(first, number):
            lanes = pl.ds(first * 256, 256)
            return spread(
                where,
                lambda peer: part.at[peer, :, lanes],
                lambda lat: part_got.at[lat, :, lanes],
                lat_sems.at[number],
            )

        merge(0, 0)
        flights.start("part_0", half(0, 2))
        merge(1, 0)
        flights.start("part_1", half(1, 3))
        part_got[where.lat] = part[where.lat]
        slices_t[...] = own_rows.astype(F32).T.astype(BF16)
        flights.wait("part_0")
        flights.wait("part_1")
        coarse_ref[...] = unfold_one(sum_slots(part_got))
        packed[...] = fold_one(group_stats(coarse_ref[...], 0, 2048)[0]).astype(BF16)

        def gather_half(src, first, number):
            lanes = pl.ds(first * 256, 256)
            return spread(
                where,
                lambda peer: src.at[:, lanes],
                lambda lat: normed_got.at[lat, :, lanes],
                lat_sems.at[number],
            )

        def rows_half(first):
            parts = unfold(normed_got[:, :, first * 256 : first * 256 + 256].astype(F32))
            for n in range(4):
                lanes = slice(n * 512 + first * 256, n * 512 + first * 256 + 256)
                rows[:, lanes] = parts[n].reshape(LATS * CELL, 256).astype(BF16)
                yield lanes

        for first in range(2):
            flights.start(f"normed_{first}", gather_half(packed, first, (4, 14)[first]))
        normed_got[where.lat] = packed[...]
        flights.wait("w_qkv_c")
        sums = [jnp.zeros((LATS * CELL, 256), F32)] * 3
        for first in range(2):
            flights.wait(f"normed_{first}")
            for lanes in rows_half(first):
                for m in range(3):
                    sums[m] = sums[m] + mm(rows[:, lanes], w_qkv_c[m, lanes])
        for m in range(3):
            qkv[m] = sums[m].astype(BF16)
        real_c = key % CELL < 36

        def window_c(w, carry):
            own_rows = pl.ds(pl.multiple_of(w * WIN, WIN), WIN)
            heads = stack_heads(qkv[0, own_rows], masks)
            d_heads = stack_heads(d_mixed_c[own_rows], masks)
            scores = mm_nt(heads, qkv[1, own_rows]) * 0.125
            weights = softmax_rows(jnp.where(real_c, scores, -1e30))
            weights_bf = weights.astype(BF16)
            mixed_c[own_rows] = pick_heads(mm(weights_bf, qkv[2, own_rows]), masks).astype(BF16)
            d_scores = scores_back(weights, mm_nt(d_heads, qkv[2, own_rows]))
            d_qkv[own_rows, :256] = pick_heads(mm(d_scores, qkv[1, own_rows]), masks).astype(BF16)
            d_qkv[own_rows, 256:512] = mm_tn(d_scores, heads).astype(BF16)
            d_qkv[own_rows, 512:] = mm_tn(weights_bf, d_heads).astype(BF16)
            return carry

        lax.fori_loop(0, 4, window_c, 0, unroll=2)

        def back(c, carry):
            quarters = []
            for n in range(4):
                part_rows = pl.ds(pl.multiple_of(n * 512 + c * 256, 256), 256)
                d_rows = mm_nt(d_qkv[:, :256], w_qkv_c[0, part_rows])
                d_rows = d_rows + mm_nt(d_qkv[:, 256:512], w_qkv_c[1, part_rows])
                d_rows = d_rows + mm_nt(d_qkv[:, 512:], w_qkv_c[2, part_rows])
                quarters.append(d_rows.reshape(LATS, CELL, 256))
            part[:, :, pl.ds(pl.multiple_of(c * 256, 256), 256)] = fold(quarters).astype(BF16)
            return carry

        back(0, 0)
        flights.start("d_part_0", half(0, 5))
        back(1, 0)
        flights.start("d_part_1", half(1, 6))
        part_got[where.lat] = part[where.lat]
        rows_t[...] = rows[...].astype(F32).T.astype(BF16)
        mixed_t = mixed_c[...].astype(F32).T.astype(BF16)

        def shares(m, carry):
            grad = mm(mixed_t, cot_rows[:, pl.ds(pl.multiple_of(m * 256, 256), 256)]).astype(BF16)
            for c in range(2):
                share[c, m // 2, m % 2, :256] = grad[:, c * 128 : c * 128 + 128]
                own_rows = pl.ds(pl.multiple_of(m * 256 + c * 128, 128), 128)
                grad_qkv = mm(rows_t[own_rows], d_qkv[...]).astype(BF16)
                for n in range(6):
                    share[c, m // 2, m % 2, 256 + 128 * n : 384 + 128 * n] = grad_qkv[
                        :, 128 * n : 128 * n + 128
                    ]
            return carry

        lax.fori_loop(0, 8, shares, 0)
        flights.start(
            "core_a",
            [remote(share.at[1 - core], core_a, share_sems.at[0, 0], share_sems.at[1, 0], sibling)],
        )

        def add_pairs(got):
            def add(n, carry):
                got[n] = (share[core, n].astype(F32) + got[n].astype(F32)).astype(BF16)
                return carry

            lax.fori_loop(0, 4, add, 0)

        def z_copies(src, dst, sems):
            copies = []
            for a in range(1, 4):
                there = lax.rem(z + a, 4)
                copies.append(
                    remote(
                        src.at[there], dst.at[a], sems.at[0, a], sems.at[1, a],
                        where.lon_at(there, y, core),
                    )
                )
            return copies

        flights.wait("d_part_0")
        flights.wait("d_part_1")
        d_normed = unfold_one(sum_slots(part_got).astype(BF16).astype(F32))
        d_coarse = fold_one(group_pullback(coarse_ref[...], d_normed, 0, 2048))
        d_packed[...] = (cot[...].astype(F32) + d_coarse).astype(BF16)
        for first in range(2):
            flights.start(f"d_coarse_{first}", gather_half(d_packed, first, (7, 15)[first]))
        normed_got[where.lat] = d_packed[...]
        flights.wait("core_a")
        add_pairs(core_a)
        flights.start("z_a", z_copies(core_a, z_a, z_sems.at[0]))
        sums = [jnp.zeros((LATS * CELL, 512), F32)] * 2
        for first in range(2):
            flights.wait(f"d_coarse_{first}")
            for lanes in rows_half(first):
                for n in range(2):
                    sums[n] = sums[n] + mm_nt(rows[:, lanes], w_merge[n * 512 : n * 512 + 512, lanes])
        merged[...] = pack(*sums)
        flights.start(
            "d_slices",
            spread(where, lambda peer: merged.at[peer], lambda lat: slices.at[lat], lat_sems.at[8]),
        )
        slices[where.lat] = merged[where.lat]

        def merge_shares(m, carry):
            grad = mm(slices_t[...], rows[:, pl.ds(pl.multiple_of(m * 256, 256), 256)]).astype(BF16)
            for c in range(2):
                share[c, m // 2, m % 2] = grad[:, c * 128 : c * 128 + 128]
            return carry

        lax.fori_loop(0, 8, merge_shares, 0)
        flights.start(
            "core_b",
            [remote(share.at[1 - core], core_b, share_sems.at[0, 1], share_sems.at[1, 1], sibling)],
        )
        flights.wait("d_slices")

        d_gathered = group_pullback(
            blended[...].reshape(16, CELL, E),
            slices[...].astype(F32).reshape(16, CELL, E),
            0,
            16 * E,
        )
        flights.wait("cot_fine")
        blended[...] = mm(to_cells[...], grid_in[...]) + d_gathered.reshape(16 * CELL, E)
        d_bf = blended[...].astype(BF16)
        send_in[...] = mm(in_send[...], d_bf).astype(BF16)
        flights.start("halo3", halo_copies(where, -1, send_in, got_in2, halo_sems.at[2]))
        own = mm(in_own[...], d_bf)
        flights.wait("core_b")
        add_pairs(core_b)
        flights.wait("z_a")
        z_a[0] = core_a[z]
        line_a[...] = sum_slots(z_a).astype(BF16)
        flights.start("z_b", z_copies(core_b, z_b, z_sems.at[1]))
        flights.start(
            "y_a", [remote(line_a.at[1 - y], y_a, share_sems.at[0, 2], share_sems.at[1, 2], other_y)]
        )
        flights.wait("halo3")
        d_out = (own + mm(in_halo[...], got_in2[...])).astype(BF16)
        grad = mm_tn(mixed_f[...], d_out).astype(BF16)
        for c in range(2):
            fine_0[:, :, c] = grad[:, c * 256 : c * 256 + 256].reshape(2, 8, 32, 256)
        mixed_f[...] = mm_nt(d_out, w_proj_f[...]).astype(BF16)

        def window_b(g):
            lanes = slice(g * 256, g * 256 + 256)

            def step(w, carry):
                own_rows = pl.ds(pl.multiple_of(w * WIN, WIN), WIN)
                weights = probs[w * 2 + g]
                heads = stack_heads(q[own_rows, lanes], masks)
                d_heads = stack_heads(mixed_f[own_rows, lanes], masks)
                d_scores = scores_back(weights, mm_nt(d_heads, v[own_rows, lanes]))
                new_q = pick_heads(mm(d_scores, k[own_rows, lanes]), masks).astype(BF16)
                new_k = mm_tn(d_scores, heads).astype(BF16)
                v[own_rows, lanes] = mm_tn(weights.astype(BF16), d_heads).astype(BF16)
                q[own_rows, lanes] = new_q
                k[own_rows, lanes] = new_k
                return carry

            return step

        def to_core(name, fine, pair, sems):
            flights.start(
                name, [remote(fine.at[1 - core], pair, sems.at[0], sems.at[1], sibling)]
            )

        def add_core(fine, pair):
            pair[...] = (fine[core].astype(F32) + pair[...].astype(F32)).astype(BF16)

        def to_lat(name, pair, got, sems):
            flights.start(name, spread(where, lambda peer: pair.at[peer], lambda lat: got.at[lat], sems))
            got[where.lat] = pair[where.lat]

        def to_y(name, piece, half, sems):
            flights.start(name, [remote(piece, half, sems.at[0], sems.at[1], other_y)])

        def to_z(name, piece, half, got, sems):
            half[...] = (piece[...].astype(F32) + half[...].astype(F32)).astype(BF16)
            copies = []
            for n in range(1, 4):
                there = where.lon_at(lax.rem(z + n, 4), y, core)
                copies.append(remote(half, got.at[z], sems.at[0, n], sems.at[1, n], there))
            flights.start(name, copies)
            got[z] = half[...]

        def to_all(name, src, dst_of, sems, pass_sems):
            copies = spread(where, lambda peer: src, dst_of, sems)
            for copy in copies:
                copy.start()

            def to_sibling(n):
                rows_of = dst_of(lax.rem(where.lat - n + LATS, LATS))
                return remote(rows_of, rows_of, pass_sems.at[0, n], pass_sems.at[1, n], sibling)

            passed = [to_sibling(n) for n in range(LATS)]
            passed[0].start()

            def finish():
                for n in range(1, LATS):
                    copies[n - 1].wait()
                    passed[n].start()
                for copy in passed:
                    copy.wait()

            return finish

        def shard(lat):
            return pl.ds(pl.multiple_of(core * 256 + lat * 32, 32), 32)

        def qkv_half(g):
            return lambda lat: grad_qkv_f.at[:, shard(lat), pl.ds(g * 256, 256)]

        lax.fori_loop(0, 8, window_b(0), 0, unroll=2)
        x_t = x[...].astype(F32).T.astype(BF16)
        for m, ref in enumerate((q, k, v)):
            fine_0[:, :, 2 + m] = mm(x_t, ref[:, :256]).astype(BF16).reshape(2, 8, 32, 256)
        to_core("core_0", fine_0, pair_0, core_sems.at[0])
        lax.fori_loop(0, 4, window_b(1), 0, unroll=2)
        flights.wait("core_0")
        add_core(fine_0, pair_0)
        to_lat("lat_0", pair_0, lat_0, lat_sems.at[9])
        lax.fori_loop(4, 8, window_b(1), 0, unroll=2)
        for m, ref in enumerate((q, k, v)):
            fine_1[:, :, m] = mm(x_t, ref[:, 256:]).astype(BF16).reshape(2, 8, 32, 256)
        to_core("core_1", fine_1, pair_1, core_sems.at[1])
        d_shifted = mm_nt(q[...], w_qkv_f[0]) + mm_nt(k[...], w_qkv_f[1])
        d_shifted = (d_shifted + mm_nt(v[...], w_qkv_f[2])).astype(BF16)
        send_out[...] = mm(out_send[...], d_shifted).astype(BF16)
        flights.start("halo4", halo_copies(where, 1, send_out, got_out2, halo_sems.at[3]))
        flights.wait("core_1")
        add_core(fine_1, pair_1)
        to_lat("lat_1", pair_1, lat_1, lat_sems.at[10])
        flights.wait("lat_0")
        piece_0[...] = sum_slots(lat_0).astype(BF16)
        to_y("y_0", piece_0, half_0, core_sems.at[2])
        own = mm(out_own[...], d_shifted)
        flights.wait("y_0")
        to_z("lon_0", piece_0, half_0, lon_0, lon_sems.at[0])
        flights.wait("halo4")
        d_normed = (own + mm(out_halo[...], got_out2[...])).astype(BF16).astype(F32)
        grad = blended[...] + pullback(tg[...].astype(F32), d_normed)
        flights.wait("to_grid")
        grad_tokens[...] = mm(to_grid[...], grad.astype(BF16)).astype(BF16)
        flights.wait("lat_1")
        piece_1[...] = sum_slots(lat_1).astype(BF16)
        to_y("y_1", piece_1, half_1, core_sems.at[3])
        flights.wait("lon_0")
        piece_0[...] = sum_slots(lon_0).astype(BF16)
        grad_qkv_f[:, shard(where.lat), :256] = piece_0[2:]
        grad_proj_f[:, shard(where.lat)] = piece_0[:2]
        ends = [
            to_all("qkv_0", piece_0.at[pl.ds(2, 3)], qkv_half(0), lat_sems.at[11], pass_sems.at[0]),
            to_all(
                "proj", piece_0.at[pl.ds(0, 2)], lambda lat: grad_proj_f.at[:, shard(lat)],
                lat_sems.at[12], pass_sems.at[1],
            ),
        ]
        flights.wait("y_1")
        to_z("lon_1", piece_1, half_1, lon_1, lon_sems.at[1])
        flights.wait("z_b")
        z_b[0] = core_b[z]
        line_b[...] = sum_slots(z_b).astype(BF16)
        flights.start(
            "y_b", [remote(line_b.at[1 - y], y_b, share_sems.at[0, 3], share_sems.at[1, 3], other_y)]
        )
        flights.wait("lon_1")
        piece_1[...] = sum_slots(lon_1).astype(BF16)
        grad_qkv_f[:, shard(where.lat), 256:] = piece_1[...]
        ends.append(to_all("qkv_1", piece_1, qkv_half(1), lat_sems.at[13], pass_sems.at[2]))
        flights.wait("y_a")
        grad_proj_c[...] = line_a[y, :256].astype(F32) + y_a[:256].astype(F32)
        for n in range(6):
            own_rows = slice(256 + 128 * n, 384 + 128 * n)
            grad_qkv_c[n // 2, :, (n % 2) * 128 : (n % 2) * 128 + 128] = line_a[y, own_rows].astype(
                F32
            ) + y_a[own_rows].astype(F32)
        flights.wait("y_b")
        grad_merge[...] = line_b[y].astype(F32) + y_b[...].astype(F32)
        for end in ends:
            end()

    body()


def dma(*shape):
    return pltpu.SemaphoreType.DMA(shape)


def bf(*shape):
    return pltpu.VMEM(shape, BF16)


def f32(*shape):
    return pltpu.VMEM(shape, F32)


def per_device(tokens, w_qkv_f, w_proj_f, w_merge, w_qkv_c, w_proj_c, cot_fine, cot_coarse):
    to_cells, in_send, in_own, in_halo, out_send, out_own, out_halo, to_grid = tables()
    flat = tokens.reshape(ROWS * COLS, E)
    cot_flat = cot_fine.reshape(ROWS * COLS, E)
    size = 16 * CELL
    wide = (LATS, 144, E)
    slim = (LATS, WIN, E)
    near = pl.BlockSpec(memory_space=pltpu.VMEM)
    far = pl.BlockSpec(memory_space=pl.ANY)
    shares = [bf(4, 2, 1024, 128)] * 2 + [bf(2, 1024, 128), bf(1024, 128)]
    grad_tokens, grad_qkv_f, grad_proj_f, grad_merge, grad_qkv_c, grad_proj_c = pl.pallas_call(
        whole,
        out_shape=[
            jax.ShapeDtypeStruct((ROWS * COLS, E), BF16),
            jax.ShapeDtypeStruct((3, E, E), BF16),
            jax.ShapeDtypeStruct((2, E, 256), BF16),
            jax.ShapeDtypeStruct((1024, 128), F32),
            jax.ShapeDtypeStruct((3, 128, 256), F32),
            jax.ShapeDtypeStruct((256, 128), F32),
        ],
        in_specs=[near] + [far] * 15,
        out_specs=[near] * 6,
        scratch_shapes=[
            *[bf(*t.shape) for t in (to_cells, in_send, in_own, in_halo)],
            *[bf(*t.shape) for t in (out_send, out_own, out_halo, to_grid, cot_flat)],
            *[bf(*t.shape) for t in (w_qkv_f, w_proj_f, w_merge, w_qkv_c, w_proj_c)],
            *[bf(size, E)] * 4, f32(16, 4 * WIN, WIN), bf(size, E), bf(size, E), f32(size, E),
            bf(*slim), bf(*slim),
            *[bf(224, E)] * 6,
            bf(144, E), bf(*wide), bf(*wide), f32(4, CELL, E), bf(144, E), bf(*wide), bf(320, 2048), bf(2048, 320),
            bf(320, 2048), bf(3, 320, 256), bf(320, 256), bf(320, 256), bf(320, 768),
            bf(144, E), bf(1024, 320),
            bf(2, 4, 2, 1024, 128), *shares, *shares,
            bf(2, 8, 5, 32, 256), *[bf(8, 5, 32, 256)] * 2, bf(4, 5, 32, 256), *[bf(5, 32, 256)] * 2,
            bf(2, 8, 3, 32, 256), *[bf(8, 3, 32, 256)] * 2, bf(4, 3, 32, 256), *[bf(3, 32, 256)] * 2,
            dma(14), dma(4, 2, 3), dma(16, 2, LATS), dma(2, 4), dma(2, 2, 4), dma(4, 2), dma(2, 2, 4),
            dma(3, 2, LATS),
        ],
        compiler_params=pltpu.CompilerParams(
            collective_id=1, has_side_effects=True, vmem_limit_bytes=VMEM_BYTES
        ),
    )(
        cot_coarse[0], flat, to_cells, in_send, in_own, in_halo, out_send, out_own, out_halo, to_grid, cot_flat,
        w_qkv_f, w_proj_f, w_merge, w_qkv_c, w_proj_c,
    )
    arrays = (grad_tokens, grad_qkv_f, grad_proj_f, grad_merge, grad_qkv_c, grad_proj_c)
    outs = [(ROWS * COLS, E), (3, E, E), (E, E), (1024, 128), (3, 128, 256), (256, 128)]
    steps = 4

    def cut(shape, dim):
        size = tuple(s // steps if d == dim else s for d, s in enumerate(shape))
        return pl.BlockSpec(size, lambda i: tuple(i if d == dim else 0 for d in range(len(shape))))

    dims = (0, 1, 0, 0, 1, 0)
    results = pl.pallas_call(
        finish,
        grid=(steps,),
        out_shape=[jax.ShapeDtypeStruct(s, F32 if n else BF16) for n, s in enumerate(outs)],
        in_specs=[cut(t.shape, 1 if n == 2 else d) for n, (t, d) in enumerate(zip(arrays, dims))],
        out_specs=[cut(s, d) for s, d in zip(outs, dims)],
    )(*arrays)
    return (results[0].reshape(tokens.shape), *results[1:])


def finish(tokens, qkv_f, proj_f, merge, qkv_c, proj_c, *outs):
    fine_scale, coarse_scale = 73728**-0.5, 4608**-0.5
    outs[0][...] = tokens[...]
    outs[1][...] = qkv_f[...].astype(F32) * fine_scale
    outs[2][:, :256] = proj_f[0].astype(F32) * fine_scale
    outs[2][:, 256:] = proj_f[1].astype(F32) * fine_scale
    for source, out in zip((merge, qkv_c, proj_c), outs[3:]):
        out[...] = source[...] * coarse_scale


def solution(mesh):
    return jax.shard_map(
        per_device,
        mesh=mesh,
        in_specs=(
            P(None, "lat", "lon", None),
            P(),
            P(),
            P("lat", None),
            P(None, None, "lat"),
            P("lat", None),
            P(None, "lat", "lon", None),
            P(None, "lat", "lon", None),
        ),
        out_specs=(
            P(None, "lat", "lon", None),
            P(),
            P(),
            P("lat", "lon"),
            P(None, "lon", "lat"),
            P("lat", "lon"),
        ),
        check_vma=False,
    )
```

profile of v0, /device:TPU:1, one launch (start us, length us, event | category | flops | bytes accessed | tf_op | source)
XLA Modules:
  0.0 194.5 jit_solution(13950469101422970115)
XLA Ops:
  0.6 188.7 %shard_map.199 = (bf16[576,512]{1,0:T(8,128)(2,1)}, bf16[3,512,512]{2,1,0:T(8,128)(2,1)}, bf16[2,512,256]{2,1,0:T(8,128)(2,1)}, f32[1024,128]{1,0:T(8,128)}, f32[3,128,256]{2,1,0:T(8,128)}, /*index=5*/f32[256,128]{1,0:T(8,128)}) custom-call(bf16[3,12,2048]{2,1,0:T(8,128)(2,1)} %bitcast.6, bf16[576,512]{1,0:T(8,128)(2,1)} %bitcast.4, ...), custom_call_target="tpu_custom_call" | custom-call | tf_op jit(solution)/shard_map/pallas_call | solution.py:778
  189.3 5.0 %shard_map.200 = (bf16[576,512]{1,0:T(8,128)(2,1)}, f32[3,512,512]{2,1,0:T(8,128)}, f32[512,512]{1,0:T(8,128)}, f32[1024,128]{1,0:T(8,128)}, f32[3,128,256]{2,1,0:T(8,128)}, /*index=5*/f32[256,128]{1,0:T(8,128)}) custom-call(bf16[576,512]{1,0:T(8,128)(2,1)} %get-tuple-element.18.tokens, bf16[3,512,512]{2,1,0:T(8,128)(2,1)} %get-tuple-element.19.qkv_f, ...), custom_call_target="tpu_custom_call" | custom-call | tf_op jit(solution)/shard_map/pallas_call | solution.py:822
where the time goes:
time: 195 us
  Pallas kernels  194 us (99%)
    pallas_call x1, Pallas kernels, per_device(): pl.pallas_call(whole, out_shape=[jax.ShapeDtypeStruct((ROWS * COLS, E), B...  189 us
    pallas_call x1, Pallas kernels, per_device(): pl.pallas_call(finish, grid=(steps,), out_shape=[jax.ShapeDtypeStruct(s,...  5.02 us

commit v1 on v0

--- a/solution.py
+++ b/solution.py
@@ -312,6 +312,7 @@
     d_packed, slices_t,
     share, core_a, z_a, line_a, y_a,
     core_b, z_b, line_b, y_b,
+    fine_p, pair_p, lat_p, lon_p, piece_p, half_p,
     fine_0, pair_0, lat_0, lon_0, piece_0, half_0, fine_1, pair_1, lat_1, lon_1, piece_1, half_1,
     load_sems, halo_sems, lat_sems, share_sems, z_sems, core_sems, lon_sems, pass_sems,
 ):
@@ -609,7 +610,7 @@
         d_out = (own + mm(in_halo[...], got_in2[...])).astype(BF16)
         grad = mm_tn(mixed_f[...], d_out).astype(BF16)
         for c in range(2):
-            fine_0[:, :, c] = grad[:, c * 256 : c * 256 + 256].reshape(2, 8, 32, 256)
+            fine_p[:, :, c] = grad[:, c * 256 : c * 256 + 256].reshape(2, 8, 32, 256)
         mixed_f[...] = mm_nt(d_out, w_proj_f[...]).astype(BF16)
 
         def window_b(g):
@@ -681,16 +682,23 @@
         def qkv_half(g):
             return lambda lat: grad_qkv_f.at[:, shard(lat), pl.ds(g * 256, 256)]
 
+        to_core("core_p", fine_p, pair_p, core_sems.at[4])
         lax.fori_loop(0, 8, window_b(0), 0, unroll=2)
+        flights.wait("core_p")
+        add_core(fine_p, pair_p)
+        to_lat("lat_p", pair_p, lat_p, lat_sems.at[16])
         x_t = x[...].astype(F32).T.astype(BF16)
         for m, ref in enumerate((q, k, v)):
-            fine_0[:, :, 2 + m] = mm(x_t, ref[:, :256]).astype(BF16).reshape(2, 8, 32, 256)
+            fine_0[:, :, m] = mm(x_t, ref[:, :256]).astype(BF16).reshape(2, 8, 32, 256)
         to_core("core_0", fine_0, pair_0, core_sems.at[0])
         lax.fori_loop(0, 4, window_b(1), 0, unroll=2)
         flights.wait("core_0")
         add_core(fine_0, pair_0)
         to_lat("lat_0", pair_0, lat_0, lat_sems.at[9])
         lax.fori_loop(4, 8, window_b(1), 0, unroll=2)
+        flights.wait("lat_p")
+        piece_p[...] = sum_slots(lat_p).astype(BF16)
+        to_y("y_p", piece_p, half_p, core_sems.at[5])
         for m, ref in enumerate((q, k, v)):
             fine_1[:, :, m] = mm(x_t, ref[:, 256:]).astype(BF16).reshape(2, 8, 32, 256)
         to_core("core_1", fine_1, pair_1, core_sems.at[1])
@@ -701,12 +709,23 @@
         flights.wait("core_1")
         add_core(fine_1, pair_1)
         to_lat("lat_1", pair_1, lat_1, lat_sems.at[10])
+        flights.wait("y_p")
+        to_z("lon_p", piece_p, half_p, lon_p, lon_sems.at[2])
         flights.wait("lat_0")
         piece_0[...] = sum_slots(lat_0).astype(BF16)
         to_y("y_0", piece_0, half_0, core_sems.at[2])
         own = mm(out_own[...], d_shifted)
         flights.wait("y_0")
         to_z("lon_0", piece_0, half_0, lon_0, lon_sems.at[0])
+        flights.wait("lon_p")
+        piece_p[...] = sum_slots(lon_p).astype(BF16)
+        grad_proj_f[:, shard(where.lat)] = piece_p[...]
+        ends = [
+            to_all(
+                "proj", piece_p, lambda lat: grad_proj_f.at[:, shard(lat)],
+                lat_sems.at[12], pass_sems.at[1],
+            )
+        ]
         flights.wait("halo4")
         d_normed = (own + mm(out_halo[...], got_out2[...])).astype(BF16).astype(F32)
         grad = blended[...] + pullback(tg[...].astype(F32), d_normed)
@@ -717,15 +736,8 @@
         to_y("y_1", piece_1, half_1, core_sems.at[3])
         flights.wait("lon_0")
         piece_0[...] = sum_slots(lon_0).astype(BF16)
-        grad_qkv_f[:, shard(where.lat), :256] = piece_0[2:]
-        grad_proj_f[:, shard(where.lat)] = piece_0[:2]
-        ends = [
-            to_all("qkv_0", piece_0.at[pl.ds(2, 3)], qkv_half(0), lat_sems.at[11], pass_sems.at[0]),
-            to_all(
-                "proj", piece_0.at[pl.ds(0, 2)], lambda lat: grad_proj_f.at[:, shard(lat)],
-                lat_sems.at[12], pass_sems.at[1],
-            ),
-        ]
+        grad_qkv_f[:, shard(where.lat), :256] = piece_0[...]
+        ends.append(to_all("qkv_0", piece_0, qkv_half(0), lat_sems.at[11], pass_sems.at[0]))
         flights.wait("y_1")
         to_z("lon_1", piece_1, half_1, lon_1, lon_sems.at[1])
         flights.wait("z_b")
@@ -798,9 +810,10 @@
             bf(320, 2048), bf(3, 320, 256), bf(320, 256), bf(320, 256), bf(320, 768),
             bf(144, E), bf(1024, 320),
             bf(2, 4, 2, 1024, 128), *shares, *shares,
-            bf(2, 8, 5, 32, 256), *[bf(8, 5, 32, 256)] * 2, bf(4, 5, 32, 256), *[bf(5, 32, 256)] * 2,
+            bf(2, 8, 2, 32, 256), *[bf(8, 2, 32, 256)] * 2, bf(4, 2, 32, 256), *[bf(2, 32, 256)] * 2,
             bf(2, 8, 3, 32, 256), *[bf(8, 3, 32, 256)] * 2, bf(4, 3, 32, 256), *[bf(3, 32, 256)] * 2,
-            dma(14), dma(4, 2, 3), dma(16, 2, LATS), dma(2, 4), dma(2, 2, 4), dma(4, 2), dma(2, 2, 4),
+            bf(2, 8, 3, 32, 256), *[bf(8, 3, 32, 256)] * 2, bf(4, 3, 32, 256), *[bf(3, 32, 256)] * 2,
+            dma(14), dma(4, 2, 3), dma(17, 2, LATS), dma(2, 4), dma(2, 2, 4), dma(6, 2), dma(3, 2, 4),
             dma(3, 2, LATS),
         ],
         compiler_params=pltpu.CompilerParams(

time: 195 us -> 190 us (0.974)
  Pallas kernels: 194 us -> 189 us
    pallas_call x1, Pallas kernels: 189 us -> 184 us  [per_device(): pl.pallas_call(whole, out_shape=[jax.ShapeDtypeStruct((ROWS * COLS, E), B...]
where the time goes in v1:
time: 190 us; the launch traced here: 189 us
  Pallas kernels  189 us (99%)
    pallas_call x1, Pallas kernels, per_device(): pl.pallas_call(whole, out_shape=[jax.ShapeDtypeStruct((ROWS * COLS, E), B...  184 us
    pallas_call x1, Pallas kernels, per_device(): pl.pallas_call(finish, grid=(steps,), out_shape=[jax.ShapeDtypeStruct(s,...  5.02 us

profile of v1, /device:TPU:1, one launch (start us, length us, event | category | flops | bytes accessed | tf_op | source)
XLA Modules:
  0.0 189.4 jit_solution(15016030408244886574)
XLA Ops:
  0.6 183.6 %shard_map.199 = (bf16[576,512]{1,0:T(8,128)(2,1)}, bf16[3,512,512]{2,1,0:T(8,128)(2,1)}, bf16[2,512,256]{2,1,0:T(8,128)(2,1)}, f32[1024,128]{1,0:T(8,128)}, f32[3,128,256]{2,1,0:T(8,128)}, /*index=5*/f32[256,128]{1,0:T(8,128)}) custom-call(bf16[3,12,2048]{2,1,0:T(8,128)(2,1)} %bitcast.6, bf16[576,512]{1,0:T(8,128)(2,1)} %bitcast.4, ...), custom_call_target="tpu_custom_call" | custom-call | tf_op jit(solution)/shard_map/pallas_call | solution.py:790
  184.2 5.0 %shard_map.200 = (bf16[576,512]{1,0:T(8,128)(2,1)}, f32[3,512,512]{2,1,0:T(8,128)}, f32[512,512]{1,0:T(8,128)}, f32[1024,128]{1,0:T(8,128)}, f32[3,128,256]{2,1,0:T(8,128)}, /*index=5*/f32[256,128]{1,0:T(8,128)}) custom-call(bf16[576,512]{1,0:T(8,128)(2,1)} %get-tuple-element.18.tokens, bf16[3,512,512]{2,1,0:T(8,128)(2,1)} %get-tuple-element.19.qkv_f, ...), custom_call_target="tpu_custom_call" | custom-call | tf_op jit(solution)/shard_map/pallas_call | solution.py:835

commit v2 on v1

--- a/solution.py
+++ b/solution.py
@@ -616,17 +616,23 @@
         def window_b(g):
             lanes = slice(g * 256, g * 256 + 256)
 
-            def step(w, carry):
-                own_rows = pl.ds(pl.multiple_of(w * WIN, WIN), WIN)
-                weights = probs[w * 2 + g]
-                heads = stack_heads(q[own_rows, lanes], masks)
-                d_heads = stack_heads(mixed_f[own_rows, lanes], masks)
-                d_scores = scores_back(weights, mm_nt(d_heads, v[own_rows, lanes]))
-                new_q = pick_heads(mm(d_scores, k[own_rows, lanes]), masks).astype(BF16)
-                new_k = mm_tn(d_scores, heads).astype(BF16)
-                v[own_rows, lanes] = mm_tn(weights.astype(BF16), d_heads).astype(BF16)
-                q[own_rows, lanes] = new_q
-                k[own_rows, lanes] = new_k
+            def step(batch, carry):
+                done = []
+                for n in range(4):
+                    w = batch * 4 + n
+                    own_rows = pl.ds(pl.multiple_of(w * WIN, WIN), WIN)
+                    weights = probs[w * 2 + g]
+                    heads = stack_heads(q[own_rows, lanes], masks)
+                    d_heads = stack_heads(mixed_f[own_rows, lanes], masks)
+                    d_scores = scores_back(weights, mm_nt(d_heads, v[own_rows, lanes]))
+                    new_q = pick_heads(mm(d_scores, k[own_rows, lanes]), masks).astype(BF16)
+                    new_k = mm_tn(d_scores, heads).astype(BF16)
+                    new_v = mm_tn(weights.astype(BF16), d_heads).astype(BF16)
+                    done.append((own_rows, new_q, new_k, new_v))
+                for own_rows, new_q, new_k, new_v in done:
+                    q[own_rows, lanes] = new_q
+                    k[own_rows, lanes] = new_k
+                    v[own_rows, lanes] = new_v
                 return carry
 
             return step
@@ -683,7 +689,7 @@
             return lambda lat: grad_qkv_f.at[:, shard(lat), pl.ds(g * 256, 256)]
 
         to_core("core_p", fine_p, pair_p, core_sems.at[4])
-        lax.fori_loop(0, 8, window_b(0), 0, unroll=2)
+        lax.fori_loop(0, 2, window_b(0), 0)
         flights.wait("core_p")
         add_core(fine_p, pair_p)
         to_lat("lat_p", pair_p, lat_p, lat_sems.at[16])
@@ -691,11 +697,11 @@
         for m, ref in enumerate((q, k, v)):
             fine_0[:, :, m] = mm(x_t, ref[:, :256]).astype(BF16).reshape(2, 8, 32, 256)
         to_core("core_0", fine_0, pair_0, core_sems.at[0])
-        lax.fori_loop(0, 4, window_b(1), 0, unroll=2)
+        window_b(1)(0, 0)
         flights.wait("core_0")
         add_core(fine_0, pair_0)
         to_lat("lat_0", pair_0, lat_0, lat_sems.at[9])
-        lax.fori_loop(4, 8, window_b(1), 0, unroll=2)
+        window_b(1)(1, 0)
         flights.wait("lat_p")
         piece_p[...] = sum_slots(lat_p).astype(BF16)
         to_y("y_p", piece_p, half_p, core_sems.at[5])
@@ -711,10 +717,10 @@
         to_lat("lat_1", pair_1, lat_1, lat_sems.at[10])
         flights.wait("y_p")
         to_z("lon_p", piece_p, half_p, lon_p, lon_sems.at[2])
+        own = mm(out_own[...], d_shifted)
         flights.wait("lat_0")
         piece_0[...] = sum_slots(lat_0).astype(BF16)
         to_y("y_0", piece_0, half_0, core_sems.at[2])
-        own = mm(out_own[...], d_shifted)
         flights.wait("y_0")
         to_z("lon_0", piece_0, half_0, lon_0, lon_sems.at[0])
         flights.wait("lon_p")

time: 190 us -> 189 us (level)
  no operation moved by 1% of the time
where the time goes in v2:
time: 189 us
  Pallas kernels  188 us (99%)
    pallas_call x1, Pallas kernels, per_device(): pl.pallas_call(whole, out_shape=[jax.ShapeDtypeStruct((ROWS * COLS, E), B...  183 us
    pallas_call x1, Pallas kernels, per_device(): pl.pallas_call(finish, grid=(steps,), out_shape=[jax.ShapeDtypeStruct(s,...  5.02 us

profile of v2, /device:TPU:1, one launch (start us, length us, event | category | flops | bytes accessed | tf_op | source)
XLA Modules:
  0.0 188.9 jit_solution(13790462597092243499)
XLA Ops:
  0.6 183.0 %shard_map.199 = (bf16[576,512]{1,0:T(8,128)(2,1)}, bf16[3,512,512]{2,1,0:T(8,128)(2,1)}, bf16[2,512,256]{2,1,0:T(8,128)(2,1)}, f32[1024,128]{1,0:T(8,128)}, f32[3,128,256]{2,1,0:T(8,128)}, /*index=5*/f32[256,128]{1,0:T(8,128)}) custom-call(bf16[3,12,2048]{2,1,0:T(8,128)(2,1)} %bitcast.6, bf16[576,512]{1,0:T(8,128)(2,1)} %bitcast.4, ...), custom_call_target="tpu_custom_call" | custom-call | tf_op jit(solution)/shard_map/pallas_call | solution.py:796
  183.7 5.0 %shard_map.200 = (bf16[576,512]{1,0:T(8,128)(2,1)}, f32[3,512,512]{2,1,0:T(8,128)}, f32[512,512]{1,0:T(8,128)}, f32[1024,128]{1,0:T(8,128)}, f32[3,128,256]{2,1,0:T(8,128)}, /*index=5*/f32[256,128]{1,0:T(8,128)}) custom-call(bf16[576,512]{1,0:T(8,128)(2,1)} %get-tuple-element.18.tokens, bf16[3,512,512]{2,1,0:T(8,128)(2,1)} %get-tuple-element.19.qkv_f, ...), custom_call_target="tpu_custom_call" | custom-call | tf_op jit(solution)/shard_map/pallas_call | solution.py:841
